TPU v7x, 768 devices: a whole 4x8x12 slice. The times are simulated.
768 devices in a mesh: tm: 48 (over z_lo, y), wafer: 8 (over x, core), sim: 2 (over z_hi).
Axes of the slice: x: 4, y: 8, z: 12 (z_hi: 2, z_lo: 6; z = z_hi * 6 + z_lo), core: 2. Of those that a mesh axis runs over, the one named last changes fastest.
Arguments:
- sky: bfloat16 [64, 8, 384], P('sim', 'wafer'), may hold values from -6 to 6
- taps: bfloat16 [8, 2048], P('wafer', 'sim'), may hold values from -0.125 to 0.125
- weights: float32 [8], P('wafer'), may hold values from 0.01 to 0.06
- pixels: int32 [8, 98304], P('wafer', 'tm'), may hold values from 0 to 384
- tiles: int32 [8, 768], P('wafer', 'tm'), may hold values from 0 to 7
Outputs:
- binned_sky_maps: float32 [64, 8, 384], P('sim', 'wafer')
Inputs may be any that keep to these rules, and one draw needn't show every extreme that they name: `pixels`: the value 384 marks a padded sample, which reads zero and is not binned.
All inputs are finite; a program needn't handle non-finite values.
Results may differ from a plain program's by a relative error of at most 0.0029.
Values may be sent and summed in bfloat16 or wider, within the bound.
A program may use at most 32 MiB of HBM per device.

v0:
```python
import jax
import jax.numpy as jnp
from jax import lax
from jax.sharding import PartitionSpec as P


def shifted(value, axis, steps):
    count = lax.axis_size(axis)
    initial, last = (max(0, -steps), min(count, count - steps))
    return lax.ppermute(value, axis, [(source, source + steps) for source in range(initial, last)])


def band_blocks(tap_row, taps_len):
    count = taps_len // 128 + 1
    period = 2 * taps_len + 128
    padded_row = jnp.concatenate([tap_row, jnp.zeros((period - taps_len,), tap_row.dtype)])
    repeated = jnp.tile(padded_row, 128)[: 128 * (period - 1)].reshape(128, period - 1)
    banded = repeated[:, : count * 128].reshape(128, count, 128)
    return banded.transpose(1, 0, 2)


def pixel_table(pix_row, pixel_count):
    grouped = pix_row.reshape(-1, 128)
    return (grouped[:, :, None] == jnp.arange(pixel_count, dtype=jnp.int32)[None, None, :]).astype(
        jnp.bfloat16
    )


def sample_blocks(panels, pix_row, tile_row):
    chosen = jnp.take(panels, tile_row, axis=1)
    pixel_indicator = pixel_table(pix_row, panels.shape[2])
    picked = jnp.einsum("sbp,bcp->sbc", chosen, pixel_indicator, preferred_element_type=jnp.float32)
    return picked.astype(jnp.bfloat16)


def apply_filter(extended, toeplitz_matrix, out_blocks):
    lead_blocks = toeplitz_matrix.shape[0] - 1
    blocked = extended.reshape(extended.shape[0], -1, 128)
    stacked = jnp.stack(
        [
            blocked[:, lead_blocks - start_offset : lead_blocks - start_offset + out_blocks]
            for start_offset in range(lead_blocks + 1)
        ],
        axis=2,
    )
    return jnp.einsum("sbmr,mrc->sbc", stacked, toeplitz_matrix, preferred_element_type=jnp.float32)


def per_device(sky, taps, weights, pixels, tiles):
    skies_here = sky.shape[0]
    panels = lax.all_gather(sky, "wafer", axis=1, tiled=True)
    taps_full = lax.all_gather(taps, "sim", axis=1, tiled=True)
    det_here, time_here = pixels.shape
    taps_len = taps_full.shape[1]
    lead_blocks = taps_len // 128
    block_count = time_here // 128
    tile_count = panels.shape[1]
    pixel_count = panels.shape[2]

    def sample_one(item):
        return sample_blocks(panels, item[0], item[1]).reshape(skies_here, -1)

    stream = lax.map(sample_one, (pixels, tiles))
    toeplitz_matrix = lax.map(lambda tap_row: band_blocks(tap_row, taps_len), taps_full)
    carried = jnp.zeros((det_here, skies_here, lead_blocks, 128), jnp.float32)
    previous = shifted(stream, "tm", 1)
    tile_range = jnp.arange(tile_count, dtype=jnp.int32)

    def bin_single_stream(running, item):
        stream_row, previous_row, toeplitz_one, weight_one, pix_row, tile_row, carried_row = item
        extended = jnp.concatenate([previous_row, stream_row], axis=1)
        filtered_stream = apply_filter(extended, toeplitz_one, block_count)
        filtered_stream = filtered_stream + carried_row
        weighted = (weight_one * filtered_stream).astype(jnp.bfloat16)
        pixel_indicator = pixel_table(pix_row, pixel_count)
        binned = jnp.einsum(
            "sbc,bcp->sbp", weighted, pixel_indicator, preferred_element_type=jnp.float32
        )
        tile_hot = (tile_row[:, None] == tile_range[None, :]).astype(jnp.float32)
        added = jnp.einsum("sbp,bt->stp", binned, tile_hot, precision=lax.Precision.HIGHEST)
        return (running + added, None)

    start = jnp.zeros((skies_here, tile_count, pixel_count), jnp.float32)
    running, _ = lax.scan(
        bin_single_stream,
        start,
        (stream, previous, toeplitz_matrix, weights, pixels, tiles, carried),
    )
    partial_map = lax.psum_scatter(running, "wafer", scatter_dimension=1, tiled=True)
    return lax.psum(partial_map, "tm")


def solution(mesh):
    placed = (
        P("sim", "wafer", None),
        P("wafer", "sim"),
        P("wafer"),
        P("wafer", "tm"),
        P("wafer", "tm"),
    )
    return jax.shard_map(
        per_device, mesh=mesh, in_specs=placed, out_specs=P("sim", "wafer", None), check_vma=False
    )
```

profile of v0, /device:TPU:2, one launch (start us, length us, event | category | flops | bytes accessed | tf_op | source)
XLA Modules:
  0.0 408.5 jit_solution(5974264438575105703)
XLA Ops:
  6.5 0.0 copy-start
  6.5 0.0 reduce-scatter.2.cloned.1.call-start
  6.5 0.7 fusion.63
  7.2 0.7 compare_and_fusion
  7.9 19.4 %all_gather.6 = bf16[32,8,384]{2,0,1:T(8,128)(2,1)S(1)} all-gather(bf16[32,1,384]{2,0,1:T(8,128)(2,1)} %param.5), channel_id=1, replica_groups=mesh['tm'=48,'wafer'=8,'sim'=2] {'wafer'}, dimensions={1}, use_global_device_ids=true | all-gather | bytes 221184 | tf_op jit(solution)/shard_map/all_gather | solution.py:51
  27.3 0.6 gather_fusion
  27.9 2.3 bitcast_dynamic-update-slice_fusion
  30.1 0.1 copy.15
  30.2 0.1 broadcast_in_dim.36
  30.3 1.3 collective-permute-start
  31.6 0.0 copy-done
  31.6 11.4 %all_gather.7 = bf16[1,2048]{1,0:T(2,128)(2,1)S(1)} all-gather(bf16[1,1024]{1,0:T(2,128)(2,1)S(1)} %copy-done), channel_id=1, replica_groups=mesh['tm'=48,'wafer'=8,'sim'=2] {'sim'}, dimensions={1}, use_global_device_ids=true | all-gather | bytes 6144 | tf_op jit(solution)/shard_map/all_gather | solution.py:52
  43.0 0.1 tile.14
  43.1 1.2 tile.15
  44.3 1.7 reshape.65
  46.1 0.3 copy.18
  46.4 0.3 copy.19
  47.4 0.0 collective-permute-done
  47.5 0.7 fusion.20
  48.1 0.7 fusion.23
  48.8 0.7 fusion.26
  49.5 0.7 fusion.29
  50.1 0.0 copy-start.2
  50.1 0.6 fusion.32
  50.8 0.7 fusion.35
  51.4 0.7 fusion.38
  52.1 0.7 fusion.41
  52.7 0.7 fusion.44
  53.4 0.7 fusion.47
  54.1 0.7 fusion.50
  54.7 0.7 fusion.53
  55.4 0.7 fusion.56
  56.0 0.6 fusion.17
  56.7 0.7 fusion.58
  57.3 0.7 copy_dynamic-update-slice_fusion
  58.0 0.0 copy-start.1
  58.0 0.0 copy-done.2
  58.0 3.2 fusion.4
  61.3 0.0 copy-done.1
  61.3 0.8 convolution_bitcast_fusion
  62.1 0.8 copy.21
  62.9 0.0 reduce-scatter.2.cloned.1.call-update
  63.0 36.5 %reduce-scatter.2.cloned.1.call-done = f32[32,1,384]{2,0,1:T(8,128)} async-done(((f32[32,8,384]{2,0,1:T(8,128)}), f32[32,1,384]{2,0,1:T(8,128)}) %reduce-scatter.2.cloned.1.call-update) | async-done | bytes 49168 | tf_op jit(solution)/shard_map/reduce_scatter | solution.py:89
  99.5 301.6 %psum.7 = f32[32,1,384]{2,0,1:T(8,128)S(1)} all-reduce(f32[32,1,384]{2,0,1:T(8,128)} %reduce-scatter.2.cloned.1.call-done), channel_id=1, replica_groups=mesh['tm'=48,'wafer'=8,'sim'=2] {'tm'}, use_global_device_ids=true, to_apply=%region_1.2 | all-reduce | flops 12288 | bytes 98304 | tf_op jit(solution)/shard_map/psum | solution.py:90
  401.0 0.7 copy.22
  (6 shorter events, 0.1 us)
Async XLA Ops:
  6.5 25.0 %copy-start = (bf16[1,1024]{1,0:T(2,128)(2,1)S(1)}, bf16[1,1024]{1,0:T(2,128)(2,1)}, u32[]{:S(2)}) copy-start(bf16[1,1024]{1,0:T(2,128)(2,1)} %param.6) | copy-start | bytes 6148
  6.5 92.9 %reduce-scatter.2.cloned.1.call-start = ((), (), s32[]{:S(2)}) async-start(), calls=%async_computation.1 | async-start | bytes 442368 | tf_op jit(solution)/shard_map/reduce_scatter | solution.py:89
  30.3 17.1 %collective-permute-start = (bf16[1,32,2048]{2,1,0:T(8,128)(2,1)S(1)}, bf16[1,32,2048]{2,1,0:T(8,128)(2,1)S(1)}, u32[]{:S(2)}, u32[]{:S(2)}) collective-permute-start(bf16[1,32,2048]{2,1,0:T(8,128)(2,1)S(1)} %broadcast_in_dim.36), channel_id=1, source_target_pairs={{0,16},{16,32},{32,48},{48,64},{64,80},{80,96},{96,112},{112,128},... | collective-permute-start | bytes 393224 | tf_op jit(solution)/shard_map/ppermute | solution.py:10
  50.1 7.9 %copy-start.2 = (s32[1,2048]{1,0:T(1,128)S(1)}, s32[1,2048]{1,0:T(1,128)}, u32[]{:S(2)}) copy-start(s32[1,2048]{1,0:T(1,128)} %param.8) | copy-start | bytes 24580
  58.0 3.2 copy-start.1
Sparse Core Ops, SparseCore 0:
  63.1 36.3 reduce-scatter.1
where the time goes:
time: 409 us
  blocking collectives  332 us (81%)
  waiting for transfers between devices  36.5 us (9%)
  between operations  14.2 us (3%)
  other arithmetic  11.2 us (3%)
  local copies, waits for them, and re-layouts  6.69 us (2%)
  matrix products  6.32 us (2%)
    psum x1, blocking collectives, per_device(): return lax.psum(partial_map, 'tm')  302 us
    reduce_scatter x1, waiting for transfers between devices, per_device(): lax.psum_scatter(running, 'wafer', scatter_dimension=1, tiled=True)  36.5 us
    all_gather x1, blocking collectives, per_device(): panels = lax.all_gather(sky, 'wafer', axis=1, tiled=True)  19.4 us
    all_gather x1, blocking collectives, per_device(): taps_full = lax.all_gather(taps, 'sim', axis=1, tiled=True)  11.4 us
    unnamed x15, other arithmetic  9.88 us
  transfers between devices with their start and end apart: 2, of which 1 were waited for; matrix products, arithmetic and copies ran while one was open for 1% of the time, Pallas kernels for 0%

commit v1 on v0

v1 whole, which is shorter than its diff:
```python
import functools

import jax
import jax.numpy as jnp
from jax import lax
from jax.experimental import pallas as pl
from jax.experimental.pallas import tpu as pltpu
from jax.sharding import PartitionSpec as P

MESH = pl.DeviceIdType.MESH
Y = 8
CHUNK = 256


def kernel(
    dims,
    sky_ref,
    taps_ref,
    weights_ref,
    pixels_ref,
    tiles_ref,
    out_ref,
    sky_all,
    taps_all,
    code_ref,
    prev_ref,
    onehot_ref,
    toep_ref,
    stream_ref,
    part_ref,
    core_in,
    x_out,
    x_in,
    y_out,
    y_in,
    z_out,
    z_in,
    full_ref,
    sky_sem,
    tap_sem,
    code_sem,
    core_sem,
    x_sem,
    y_sem,
    z_sem,
    g_sem,
):
    tm_count, wafer_count = dims
    z_count = tm_count // Y
    x_count = wafer_count // 2
    skies, pixel_count = sky_ref.shape
    half = taps_ref.shape[1]
    taps_len = 2 * half
    time_here = pixels_ref.shape[1]
    chunks = time_here // CHUNK
    lead = taps_len // CHUNK
    tm = lax.axis_index("tm")
    wafer = lax.axis_index("wafer")
    sim = lax.axis_index("sim")
    y, z = tm % Y, tm // Y
    x, core = wafer // 2, wafer % 2

    wafers = [{"wafer": (wafer + k) % wafer_count} for k in range(1, wafer_count)]
    other_core = {"wafer": x * 2 + 1 - core}
    xs = [(x + k) % x_count for k in range(1, x_count)]
    ys = [(y + k) % Y for k in range(1, Y)]
    zs = [(z + k) % z_count for k in range(1, z_count)]
    y_ids = [{"tm": z * Y + k} for k in ys]
    z_ids = [{"tm": k * Y + y} for k in zs]
    other_sim = {"sim": 1 - sim}

    barrier = pltpu.get_barrier_semaphore()
    partners = wafers + y_ids + z_ids + [other_sim]
    for partner in partners:
        pl.semaphore_signal(barrier, inc=1, device_id=partner, device_id_type=MESH)

    @pl.when(tm > 0)
    def _():
        pl.semaphore_signal(barrier, inc=1, device_id={"tm": tm - 1}, device_id_type=MESH)

    for block in range(time_here // 128):
        lanes = slice(block * 128, block * 128 + 128)
        code_ref[:, lanes] = pixels_ref[:, lanes] + 512 * tiles_ref[0, block]

    pl.semaphore_wait(barrier, len(partners) + (tm < tm_count - 1).astype(jnp.int32))

    sends = []

    def send(source, target, sems, index, device):
        copy = pltpu.make_async_remote_copy(
            src_ref=source,
            dst_ref=target,
            send_sem=sems.at[0, index],
            recv_sem=sems.at[1, index],
            device_id=device,
            device_id_type=MESH,
        )
        copy.start()
        sends.append(copy)
        return copy

    code_copy = pltpu.make_async_remote_copy(
        src_ref=code_ref,
        dst_ref=prev_ref,
        send_sem=code_sem.at[0],
        recv_sem=code_sem.at[1],
        device_id={"tm": (tm + 1) % tm_count},
        device_id_type=MESH,
    )

    @pl.when(tm < tm_count - 1)
    def _():
        code_copy.start()

    tap_copy = send(taps_ref, taps_all.at[sim], tap_sem, 0, other_sim)
    sky_copies = [send(sky_ref, sky_all.at[wafer], sky_sem, k, d) for k, d in enumerate(wafers)]
    sky_all[wafer] = sky_ref[...]
    taps_all[sim] = taps_ref[...]

    pixel_id = lax.broadcasted_iota(jnp.int32, (pixel_count, CHUNK), 0)

    def indicator(code):
        return jnp.where(pixel_id == (code & 511), 1.0, 0.0).astype(jnp.bfloat16)

    for n in range(chunks):
        lanes = slice(n * CHUNK, (n + 1) * CHUNK)
        onehot_ref[:, lanes] = indicator(code_ref[:, lanes])

    tap_copy.wait_recv()
    edge = jnp.zeros((1, CHUNK), jnp.float32)
    row = jnp.concatenate(
        [edge, taps_all[0].astype(jnp.float32), taps_all[1].astype(jnp.float32), edge], axis=1
    )
    spread = jnp.broadcast_to(row, (128, row.shape[1]))
    toep_ref[...] = pltpu.roll(spread, 0, 1, stride=1, stride_axis=0).astype(jnp.bfloat16)

    for copy in sky_copies:
        copy.wait_recv()
    panels = sky_all[...].reshape(wafer_count * skies, pixel_count)

    def pick(table, code):
        dense = jnp.dot(panels, table, preferred_element_type=jnp.float32)
        tile = code >> 9
        picked = dense[:skies]
        for g in range(1, wafer_count):
            picked = jnp.where(tile == g, dense[g * skies : (g + 1) * skies], picked)
        return picked.astype(jnp.bfloat16)

    for n in range(chunks):
        lanes = slice(n * CHUNK, (n + 1) * CHUNK)
        stream_ref[(lead + n) * skies : (lead + n + 1) * skies] = pick(
            onehot_ref[:, lanes], code_ref[:, lanes]
        )

    @pl.when(tm > 0)
    def _():
        code_copy.wait_recv()
        for n in range(lead):
            lanes = slice(n * CHUNK, (n + 1) * CHUNK)
            code = prev_ref[:, lanes]
            stream_ref[n * skies : (n + 1) * skies] = pick(indicator(code), code)

    @pl.when(tm == 0)
    def _():
        stream_ref[: lead * skies] = jnp.zeros((lead * skies, CHUNK), jnp.bfloat16)

    rows = chunks * skies
    windows = jnp.concatenate([stream_ref[m * skies : m * skies + rows] for m in range(lead + 1)], axis=1)
    bands = []
    for m in range(lead + 1):
        at = taps_len + CHUNK - CHUNK * m
        bands += [toep_ref[:, at : at + CHUNK], toep_ref[:, at - 128 : at - 128 + CHUNK]]
    filtered = jnp.dot(windows, jnp.concatenate(bands, axis=0), preferred_element_type=jnp.float32)
    weighted = (weights_ref[0] * filtered).astype(jnp.bfloat16)

    order = [2 * i + c for c in range(2) for i in range(x_count)]
    zero = jnp.zeros((skies, CHUNK), jnp.bfloat16)
    columns = []
    for n in range(chunks):
        tile = code_ref[:, n * CHUNK : (n + 1) * CHUNK] >> 9
        piece = weighted[n * skies : (n + 1) * skies]
        columns.append(jnp.concatenate([jnp.where(tile == g, piece, zero) for g in order], axis=0))
    part = lax.dot_general(
        jnp.concatenate(columns, axis=1),
        onehot_ref[...],
        (((1,), (1,)), ((), ())),
        preferred_element_type=jnp.float32,
    )
    part_ref[...] = part.reshape(2, x_count, skies, pixel_count)

    send(part_ref.at[1 - core], core_in, core_sem, 0, other_core).wait_recv()
    x_out[...] = part_ref[core] + core_in[...]

    copies = [
        send(x_out.at[k], x_in.at[i], x_sem, i, {"wafer": 2 * k + core}) for i, k in enumerate(xs)
    ]
    for copy in copies:
        copy.wait_recv()
    total = x_out[x]
    for i in range(x_count - 1):
        total += x_in[i]
    share = skies // Y
    for k in range(Y):
        y_out[k] = total[k * share : (k + 1) * share]

    copies = [send(y_out.at[k], y_in.at[i], y_sem, i, d) for i, (k, d) in enumerate(zip(ys, y_ids))]
    for copy in copies:
        copy.wait_recv()
    total = y_out[y]
    for i in range(Y - 1):
        total += y_in[i]
    z_out[...] = total

    copies = [send(z_out, z_in.at[i], z_sem, i, d) for i, d in enumerate(z_ids)]
    for copy in copies:
        copy.wait_recv()
    z_in[z_count - 1] = total
    total = jnp.zeros_like(total)
    for k in range(z_count):
        total += z_in[(z - k + z_count - 1) % z_count]
    full_ref[y] = total

    copies = [send(full_ref.at[y], full_ref.at[y], g_sem, i, d) for i, d in enumerate(y_ids)]
    for copy in copies:
        copy.wait_recv()
    for k in range(Y):
        out_ref[k * share : (k + 1) * share] = full_ref[k]

    for copy in sends:
        copy.wait_send()

    @pl.when(tm < tm_count - 1)
    def _():
        code_copy.wait_send()


def solution(mesh):
    tm_count, wafer_count = mesh.shape["tm"], mesh.shape["wafer"]

    def per_device(sky, taps, weights, pixels, tiles):
        skies, _, pixel_count = sky.shape
        half, time_here = taps.shape[1], pixels.shape[1]
        lead, chunks = 2 * half // CHUNK, time_here // CHUNK
        x_count, z_count, share = wafer_count // 2, tm_count // Y, skies // Y
        vmem = pl.BlockSpec(memory_space=pltpu.VMEM)
        smem = pl.BlockSpec(memory_space=pltpu.SMEM)
        f32, bf16 = jnp.float32, jnp.bfloat16
        sems = lambda n: pltpu.SemaphoreType.DMA((2, n))
        maps = pl.pallas_call(
            functools.partial(kernel, (tm_count, wafer_count)),
            out_shape=jax.ShapeDtypeStruct((skies, pixel_count), f32),
            in_specs=[vmem, vmem, smem, vmem, smem],
            out_specs=vmem,
            scratch_shapes=[
                pltpu.VMEM((wafer_count, skies, pixel_count), bf16),
                pltpu.VMEM((2, 1, half), bf16),
                pltpu.VMEM((1, time_here), jnp.int32),
                pltpu.VMEM((1, time_here), jnp.int32),
                pltpu.VMEM((pixel_count, time_here), bf16),
                pltpu.VMEM((128, 2 * half + 2 * CHUNK), bf16),
                pltpu.VMEM(((lead + chunks) * skies, CHUNK), bf16),
                pltpu.VMEM((2, x_count, skies, pixel_count), f32),
                pltpu.VMEM((x_count, skies, pixel_count), f32),
                pltpu.VMEM((x_count, skies, pixel_count), f32),
                pltpu.VMEM((x_count - 1, skies, pixel_count), f32),
                pltpu.VMEM((Y, share, pixel_count), f32),
                pltpu.VMEM((Y - 1, share, pixel_count), f32),
                pltpu.VMEM((share, pixel_count), f32),
                pltpu.VMEM((z_count, share, pixel_count), f32),
                pltpu.VMEM((Y, share, pixel_count), f32),
                sems(wafer_count - 1),
                sems(1),
                pltpu.SemaphoreType.DMA((2,)),
                sems(1),
                sems(x_count - 1),
                sems(Y - 1),
                sems(z_count - 1),
                sems(Y - 1),
            ],
            compiler_params=pltpu.CompilerParams(
                collective_id=0, has_side_effects=True, vmem_limit_bytes=40 * 1024 * 1024
            ),
        )(sky.reshape(skies, pixel_count), taps, weights, pixels, tiles)
        return maps.reshape(skies, 1, pixel_count)

    placed = (
        P("sim", "wafer", None),
        P("wafer", "sim"),
        P("wafer"),
        P("wafer", "tm"),
        P("wafer", "tm"),
    )
    return jax.shard_map(
        per_device, mesh=mesh, in_specs=placed, out_specs=P("sim", "wafer", None), check_vma=False
    )
```

time: 409 us -> 52.1 us (0.13)
  the two profiles are of different devices: /device:TPU:2 before, /device:TPU:1 now
where the time goes in v1:
time: 52.1 us; the launch traced here: 51.8 us
  Pallas kernels  47.7 us (92%)
  local copies, waits for them, and re-layouts  3.44 us (7%)
  between operations  0.67 us (1%)
    pallas_call x1, Pallas kernels, per_device(): pl.pallas_call(functools.partial(kernel, (tm_count, wafer_count)), out_sh...  47.7 us
    unnamed x8, local copies, waits for them, and re-layouts  2.77 us

profile of v1, /device:TPU:1, one launch (start us, length us, event | category | flops | bytes accessed | tf_op | source)
XLA Modules:
  0.0 51.8 jit_solution(8838144669785062972)
XLA Ops:
  0.7 0.0 copy-start.3
  0.7 0.6 %copy-done.3 = s32[1,16]{1,0:T(1,128)S(1)} copy-done((s32[1,16]{1,0:T(1,128)S(1)}, s32[1,16]{1,0:T(1,128)}, u32[]{:S(2)}) %copy-start.3) | copy-done | bytes 88
  1.3 0.0 copy-start
  1.3 0.7 %copy-done = bf16[32,1,384]{2,0,1:T(8,128)(2,1)S(1)} copy-done((bf16[32,1,384]{2,0,1:T(8,128)(2,1)S(1)}, bf16[32,1,384]{2,0,1:T(8,128)(2,1)}, u32[]{:S(2)}) %copy-start) | copy-done | bytes 24600
  2.0 0.0 copy-start.1
  2.0 0.7 %copy-done.1 = s32[1,2048]{1,0:T(1,128)S(1)} copy-done((s32[1,2048]{1,0:T(1,128)S(1)}, s32[1,2048]{1,0:T(1,128)}, u32[]{:S(2)}) %copy-start.1) | copy-done | bytes 8216
  2.7 0.0 copy-start.2
  2.7 0.7 %copy-done.2 = bf16[1,1024]{1,0:T(2,128)(2,1)S(1)} copy-done((bf16[1,1024]{1,0:T(2,128)(2,1)S(1)}, bf16[1,1024]{1,0:T(2,128)(2,1)}, u32[]{:S(2)}) %copy-start.2) | copy-done | bytes 2072
  3.4 47.7 %shard_map.55 = f32[32,384]{1,0:T(8,128)S(1)} custom-call(bf16[32,384]{1,0:T(8,128)(2,1)S(1)} %bitcast.3, bf16[1,1024]{1,0:T(2,128)(2,1)S(1)} %copy-done.2, f32[1]{0:T(128)S(6)} %copy.7.weights_ref, s32[1,2048]{1,0:T(1,128)S(1)} %copy-done.1, s32[1,16]{1,0:T(1,128)S(1)} %copy-done.3), custom_call_target="tpu_custom_call" | custom-call | tf_op jit(solution)/shard_map/pallas_call | solution.py:249
  51.2 0.7 %copy.6 = f32[32,1,384]{2,1,0:T(1,128)} copy(f32[32,1,384]{2,0,1:T(8,128)S(1)} %bitcast.2) | data formatting | bytes 98304 | tf_op jit(solution)/shard_map/reshape | solution.py:284
Async XLA Ops:
  0.7 0.7 %copy-start.3 = (s32[1,16]{1,0:T(1,128)S(1)}, s32[1,16]{1,0:T(1,128)}, u32[]{:S(2)}) copy-start(s32[1,16]{1,0:T(1,128)} %tiles_ref.1) | copy-start | bytes 196
  1.3 0.7 %copy-start = (bf16[32,1,384]{2,0,1:T(8,128)(2,1)S(1)}, bf16[32,1,384]{2,0,1:T(8,128)(2,1)}, u32[]{:S(2)}) copy-start(bf16[32,1,384]{2,0,1:T(8,128)(2,1)} %param.5) | copy-start | bytes 73732
  2.0 0.7 %copy-start.1 = (s32[1,2048]{1,0:T(1,128)S(1)}, s32[1,2048]{1,0:T(1,128)}, u32[]{:S(2)}) copy-start(s32[1,2048]{1,0:T(1,128)} %pixels_ref.1) | copy-start | bytes 24580
  2.7 0.7 %copy-start.2 = (bf16[1,1024]{1,0:T(2,128)(2,1)S(1)}, bf16[1,1024]{1,0:T(2,128)(2,1)}, u32[]{:S(2)}) copy-start(bf16[1,1024]{1,0:T(2,128)(2,1)} %taps_ref.1) | copy-start | bytes 6148

commit v2 on v1

v2 whole, which is shorter than its diff:
```python
import functools

import jax
import jax.numpy as jnp
from jax import lax
from jax.experimental import pallas as pl
from jax.experimental.pallas import tpu as pltpu
from jax.sharding import PartitionSpec as P

MESH = pl.DeviceIdType.MESH
Y = 8
CHUNK = 256
LANES = 128
Y_STEPS = (4, 3, 5, 2, 6, 1, 7)


def kernel(
    dims,
    sky_ref,
    taps_ref,
    weights_ref,
    pixels_ref,
    tiles_ref,
    out_ref,
    sky_all,
    sky_wide,
    table_ref,
    taps_all,
    weight_ref,
    pix_all,
    tile_in,
    tile_all,
    onehot_ref,
    toep_ref,
    stream_ref,
    part_ref,
    part_in,
    z_out,
    z_in,
    full_ref,
    local_sem,
    sky_sem,
    tap_sem,
    pix_sem,
    tile_sem,
    w_sem,
    z_sem,
    g_sem,
    z_ready,
    tap_ready,
):
    tm_count, wafer_count = dims
    z_count = tm_count // Y
    half_rows = sky_all.shape[1]
    share = table_ref.shape[1] // 2
    panels = sky_ref.shape[1] // LANES
    groups = panels
    half = taps_ref.shape[1]
    taps_len = 2 * half
    time_here = pixels_ref.shape[1]
    chunks = time_here // CHUNK
    lead = taps_len // CHUNK
    rows = Y * share
    tm = lax.axis_index("tm")
    wafer = lax.axis_index("wafer")
    sim = lax.axis_index("sim")
    y, z = tm % Y, tm // Y
    per_half = half_rows // share

    ws = [(wafer + k) % wafer_count for k in range(1, wafer_count)]
    ys = [(y + k) % Y for k in Y_STEPS]
    zs = [(z + k) % z_count for k in range(1, z_count)]
    w_ids = [{"wafer": k} for k in ws]
    y_ids = [{"tm": z * Y + k} for k in ys]
    z_ids = [{"tm": k * Y + y} for k in zs]

    gives_taps = z == 0
    gives_first = jnp.logical_and(gives_taps, sim == 1)
    gives_last = jnp.logical_and(gives_taps, sim == 0)
    tap_ids = [{"sim": 1 - sim, "tm": k * Y + y} for k in range(z_count)]
    tap_giver = {"sim": 1 - sim, "tm": y}
    gives_halo = jnp.logical_and(y == Y - 1, z < z_count - 1)
    halo_ids = [{"tm": (z + 1) % z_count * Y + k} for k in range(Y)]

    barrier = pltpu.get_barrier_semaphore()

    def greet(device, sem=barrier):
        pl.semaphore_signal(sem, inc=1, device_id=device, device_id_type=MESH)

    for partner in y_ids + w_ids:
        greet(partner)

    @pl.when(z > 0)
    def _():
        greet({"tm": (z - 1) * Y + Y - 1})

    @pl.when(sim == 0)
    def _():
        greet(tap_giver)

    @pl.when(gives_last)
    def _():
        for partner in tap_ids:
            greet(partner)

    for k in range(1, z_count):

        @pl.when(z + k < z_count)
        def _():
            greet({"tm": (z + k) * Y + y})

    sky_half = sky_ref.at[pl.ds(pl.multiple_of(y // per_half * half_rows, half_rows), half_rows)]
    locals_ = [
        pltpu.make_async_copy(sky_half, sky_all.at[wafer], local_sem.at[0]),
        pltpu.make_async_copy(taps_ref, taps_all.at[sim], local_sem.at[1]),
        pltpu.make_async_copy(weights_ref, weight_ref, local_sem.at[2]),
        pltpu.make_async_copy(pixels_ref, pix_all.at[y + 1], local_sem.at[3]),
        pltpu.make_async_copy(tiles_ref, tile_in.at[y + 1], local_sem.at[4]),
    ]
    for copy in locals_:
        copy.start()

    @pl.when(z == 0)
    def _():
        pix_all[0] = jnp.full((1, time_here), panels * LANES, jnp.int32)
        tile_in[0] = jnp.zeros((1, tile_in.shape[2]), jnp.int32)

    count = len(y_ids) + len(w_ids) + z
    count += jnp.where(gives_halo, Y, 0) + jnp.where(gives_first, z_count, 0) + jnp.where(sim == 1, 1, 0)
    pl.semaphore_wait(barrier, count)

    sends = []

    def remote(source, target, sems, index, device):
        return pltpu.make_async_remote_copy(
            src_ref=source,
            dst_ref=target,
            send_sem=sems.at[0, index],
            recv_sem=sems.at[1, index],
            device_id=device,
            device_id_type=MESH,
        )

    def send(*args):
        copy = remote(*args)
        copy.start()
        sends.append(copy)
        return copy

    def wait_all(copies):
        for copy in copies:
            copy.wait_recv()

    def give(source, target, sems, base, devices):
        return [
            pltpu.make_async_remote_copy(
                src_ref=source,
                dst_ref=target,
                send_sem=sems.at[0, base + i],
                recv_sem=sems.at[1, base],
                device_id=d,
                device_id_type=MESH,
            )
            for i, d in enumerate(devices)
        ]

    pix_copies = [send(pixels_ref, pix_all.at[y + 1], pix_sem, i, d) for i, d in enumerate(y_ids)]
    tile_copies = [send(tiles_ref, tile_in.at[y + 1], tile_sem, i, d) for i, d in enumerate(y_ids)]
    halo_tiles = give(tiles_ref, tile_in.at[0], tile_sem, Y - 1, halo_ids)
    halo_pixels = give(pixels_ref, pix_all.at[0], pix_sem, Y - 1, halo_ids)
    tap_copies = give(taps_ref, taps_all.at[sim], tap_sem, 0, tap_ids)

    @pl.when(gives_halo)
    def _():
        for copy in halo_tiles + halo_pixels:
            copy.start()

    @pl.when(gives_first)
    def _():
        for copy in tap_copies:
            copy.start()

    for k in range(1, z_count):

        @pl.when(z >= k)
        def _():
            greet({"tm": (z - k) * Y + y}, z_ready)

    @pl.when(sim == 1)
    def _():
        greet(tap_giver, tap_ready)

    sky_copies = [send(sky_half, sky_all.at[wafer], sky_sem, i, d) for i, d in enumerate(w_ids)]
    for copy in locals_:
        copy.wait()

    wait_all(sky_copies)
    for g in range(wafer_count):
        wide = sky_all[g].astype(jnp.float32)
        for k in range(per_half):
            sky_wide[g, k] = wide[k * share : (k + 1) * share]
    for g in range(wafer_count):
        mine = sky_wide[g, y % per_half]
        table_ref[g] = jnp.concatenate([mine, mine], axis=0)

    def spread_taps():
        tap_copies[0].wait_recv()
        edge = jnp.zeros((1, CHUNK), jnp.float32)
        row = jnp.concatenate(
            [edge, taps_all[0].astype(jnp.float32), taps_all[1].astype(jnp.float32), edge], axis=1
        )
        spread = jnp.broadcast_to(row, (LANES, row.shape[1]))
        toep_ref[...] = pltpu.roll(spread, 0, 1, stride=1, stride_axis=0).astype(jnp.bfloat16)

    taps_first = z >= z_count // 2
    pl.when(taps_first)(spread_taps)

    wait_all(tile_copies)

    @pl.when(z > 0)
    def _():
        halo_tiles[0].wait_recv()

    to_scalar = pltpu.make_async_copy(tile_in, tile_all, local_sem.at[0])
    to_scalar.start()

    lane_id = lax.broadcasted_iota(jnp.int32, (LANES, CHUNK), 0)
    def lower(pix):
        return jnp.where(pix < panels * LANES, pix & (LANES - 1), -1)

    def indicate(k):
        for n in range(chunks):
            lanes = slice(n * CHUNK, (n + 1) * CHUNK)
            low = lower(pix_all[k + 1, :, lanes])
            onehot_ref[k, :, lanes] = jnp.where(lane_id == low, 1.0, 0.0).astype(jnp.bfloat16)

    indicate(y)
    for i in reversed(range(Y - 1)):
        pix_copies[i].wait_recv()
        indicate((y + Y - Y_STEPS[i]) % Y)

    @pl.when(z > 0)
    def _():
        halo_pixels[0].wait_recv()

    to_scalar.wait()

    upper = lax.broadcasted_iota(jnp.int32, (2 * share, LANES), 0) < share

    def pick(first, block):
        lanes = slice(block * LANES, (block + 1) * LANES)
        pix = jnp.where(upper, pix_all[first, :, lanes], pix_all[first + 1, :, lanes])
        table = jnp.where(
            jnp.concatenate([upper] * panels, axis=1),
            table_ref[tile_all[first, 0, block]],
            table_ref[tile_all[first + 1, 0, block]],
        )
        low, high = pix & (LANES - 1), pix >> 7
        found = jnp.zeros((2 * share, LANES), jnp.float32)
        for j in range(panels):
            part = jnp.take_along_axis(table[:, j * LANES : (j + 1) * LANES], low, axis=1)
            found = jnp.where(high == j, part, found)
        return found

    for n in range(chunks):
        early, late = [], []
        for h in range(CHUNK // LANES):
            block = n * (CHUNK // LANES) + h
            found = [pick(2 * p + 1, block) for p in range(Y // 2)]
            turned = [pltpu.roll(f, share, 0) for f in found]
            before = [pick(0, block)]
            before += [jnp.where(upper, turned[p - 1], turned[p]) for p in range(1, Y // 2)]
            early.append(jnp.concatenate(before, axis=0))
            late.append(jnp.concatenate(found, axis=0))
        for at, halves in ((n, early), (lead + n, late)):
            stream_ref[at * rows : (at + 1) * rows] = jnp.concatenate(halves, axis=1).astype(jnp.bfloat16)

    @pl.when(gives_last)
    def _():
        pl.semaphore_wait(tap_ready, z_count)
        for copy in tap_copies:
            copy.start()

    pl.when(jnp.logical_not(taps_first))(spread_taps)

    windows = jnp.concatenate(
        [stream_ref[m * rows : (m + chunks) * rows] for m in range(lead + 1)], axis=1
    )
    bands = []
    for m in range(lead + 1):
        at = taps_len + CHUNK - CHUNK * m
        bands += [toep_ref[:, at : at + CHUNK], toep_ref[:, at - LANES : at - LANES + CHUNK]]
    filtered = jnp.dot(windows, jnp.concatenate(bands, axis=0), preferred_element_type=jnp.float32)
    weighted = (weight_ref[0, 0] * filtered).astype(jnp.bfloat16).astype(jnp.float32)

    first_group = lax.broadcasted_iota(jnp.int32, (2 * share, LANES), 0) // share
    part = jnp.zeros((wafer_count * groups * share, LANES), jnp.float32)
    for k in range(Y):
        columns = []
        for n in range(chunks):
            for h in range(CHUNK // LANES):
                block = 2 * n + h
                at = n * rows + k // 2 * 2 * share
                both = weighted[at : at + 2 * share, h * LANES : (h + 1) * LANES]
                swapped = pltpu.roll(both, share, 0)
                mine = jnp.where(upper, both, swapped) if k % 2 == 0 else jnp.where(upper, swapped, both)
                group = (pix_all[k + 1, :, block * LANES : (block + 1) * LANES] >> 7) + (
                    groups * tile_all[k + 1, 0, block]
                )
                offset = group - first_group
                columns.append(
                    jnp.concatenate(
                        [jnp.where(offset == 2 * j, mine, 0.0) for j in range(wafer_count * groups // 2)],
                        axis=0,
                    ).astype(jnp.bfloat16)
                )
        part += lax.dot_general(
            jnp.concatenate(columns, axis=1),
            onehot_ref[k],
            (((1,), (1,)), ((), ())),
            preferred_element_type=jnp.float32,
        )
    for k in range(wafer_count * groups):
        part_ref[k // groups, k % groups] = part[k * share : (k + 1) * share]

    copies = [send(part_ref.at[k], part_in.at[i], w_sem, i, d) for i, (k, d) in enumerate(zip(ws, w_ids))]
    wait_all(copies)
    total = part_ref[wafer]
    for i in range(wafer_count - 1):
        total += part_in[i]
    z_out[...] = total

    @pl.when(z < z_count - 1)
    def _():
        pl.semaphore_wait(z_ready, z_count - 1 - z)

    wait_all([send(z_out, z_in.at[i], z_sem, i, d) for i, d in enumerate(z_ids)])
    z_in[z_count - 1] = total
    total = jnp.zeros_like(total)
    for k in range(z_count):
        total += z_in[(z - k + z_count - 1) % z_count]
    full_ref[y] = total

    wait_all([send(full_ref.at[y], full_ref.at[y], g_sem, i, d) for i, d in enumerate(y_ids)])
    for k in range(Y):
        for j in range(panels):
            out_ref[k * share : (k + 1) * share, j * LANES : (j + 1) * LANES] = full_ref[k, j]

    for copy in sends:
        copy.wait_send()

    @pl.when(gives_halo)
    def _():
        for copy in halo_tiles + halo_pixels:
            copy.wait_send()

    @pl.when(gives_taps)
    def _():
        for copy in tap_copies:
            copy.wait_send()


def solution(mesh):
    tm_count, wafer_count = mesh.shape["tm"], mesh.shape["wafer"]

    def per_device(sky, taps, weights, pixels, tiles):
        skies, _, pixel_count = sky.shape
        half, time_here, blocks = taps.shape[1], pixels.shape[1], tiles.shape[1]
        lead, chunks = 2 * half // CHUNK, time_here // CHUNK
        z_count, share = tm_count // Y, skies // Y
        hbm = pl.BlockSpec(memory_space=pltpu.HBM)
        f32, bf16, i32 = jnp.float32, jnp.bfloat16, jnp.int32
        piece = (pixel_count // LANES, share, LANES)
        sems = lambda n: pltpu.SemaphoreType.DMA((2, n))
        maps = pl.pallas_call(
            functools.partial(kernel, (tm_count, wafer_count)),
            out_shape=jax.ShapeDtypeStruct((skies, pixel_count), f32),
            in_specs=[hbm] * 5,
            out_specs=pl.BlockSpec(memory_space=pltpu.VMEM),
            scratch_shapes=[
                pltpu.VMEM((wafer_count, 16, pixel_count), bf16),
                pltpu.VMEM((wafer_count, 16 // share, share, pixel_count), f32),
                pltpu.VMEM((wafer_count, 2 * share, pixel_count), f32),
                pltpu.VMEM((2, 1, half), bf16),
                pltpu.SMEM((1, 1), f32),
                pltpu.VMEM((Y + 1, 1, time_here), i32),
                pltpu.VMEM((Y + 1, 1, blocks), i32),
                pltpu.SMEM((Y + 1, 1, blocks), i32),
                pltpu.VMEM((Y, LANES, time_here), bf16),
                pltpu.VMEM((LANES, 2 * half + 2 * CHUNK), bf16),
                pltpu.VMEM(((lead + chunks) * skies, CHUNK), bf16),
                pltpu.VMEM((wafer_count,) + piece, f32),
                pltpu.VMEM((wafer_count - 1,) + piece, f32),
                pltpu.VMEM(piece, f32),
                pltpu.VMEM((z_count,) + piece, f32),
                pltpu.VMEM((Y,) + piece, f32),
                pltpu.SemaphoreType.DMA((5,)),
                sems(wafer_count - 1),
                sems(z_count),
                sems(2 * Y - 1),
                sems(2 * Y - 1),
                sems(wafer_count - 1),
                sems(z_count - 1),
                sems(Y - 1),
                pltpu.SemaphoreType.REGULAR,
                pltpu.SemaphoreType.REGULAR,
            ],
            compiler_params=pltpu.CompilerParams(
                collective_id=0, has_side_effects=True, vmem_limit_bytes=60 * 1024 * 1024
            ),
        )(sky.reshape(skies, pixel_count), taps, weights.reshape(1, 1), pixels, tiles)
        return maps.reshape(skies, 1, pixel_count)

    placed = (
        P("sim", "wafer", None),
        P("wafer", "sim"),
        P("wafer"),
        P("wafer", "tm"),
        P("wafer", "tm"),
    )
    return jax.shard_map(
        per_device, mesh=mesh, in_specs=placed, out_specs=P("sim", "wafer", None), check_vma=False
    )
```

time: 52.1 us -> 41.1 us (0.79)
  Pallas kernels: 47.7 us -> 38.8 us
  local copies, waits for them, and re-layouts: 3.44 us -> 1.47 us
    pallas_call x1, Pallas kernels: 47.7 us -> 38.8 us  [per_device(): pl.pallas_call(functools.partial(kernel, (tm_count, wafer_count)), out_sh...]
    unnamed x8 -> x0, local copies, waits for them, and re-layouts: 2.77 us -> none
    reshape x1, local copies, waits for them, and re-layouts: 0.67 us -> 1.47 us  [per_device(): return maps.reshape(skies, 1, pixel_count)]
where the time goes in v2:
time: 41.1 us; the launch traced here: 40.9 us
  Pallas kernels  38.8 us (94%)
  local copies, waits for them, and re-layouts  1.47 us (4%)
  between operations  0.66 us (2%)
    pallas_call x1, Pallas kernels, per_device(): pl.pallas_call(functools.partial(kernel, (tm_count, wafer_count)), out_sh...  38.8 us
    reshape x1, local copies, waits for them, and re-layouts, per_device(): return maps.reshape(skies, 1, pixel_count)  1.47 us

profile of v2, /device:TPU:1, one launch (start us, length us, event | category | flops | bytes accessed | tf_op | source)
XLA Modules:
  0.0 40.9 jit_solution(10792641127726217199)
XLA Ops:
  0.7 38.8 %shard_map.55 = f32[32,384]{1,0:T(8,128)} custom-call(bf16[32,384]{1,0:T(8,128)(2,1)} %bitcast.5, bf16[1,1024]{1,0:T(2,128)(2,1)} %taps_ref.1, f32[1,1]{1,0:T(1,128)} %bitcast.3.weights_ref, s32[1,2048]{1,0:T(1,128)} %pixels_ref.1, s32[1,16]{1,0:T(1,128)} %tiles_ref.1), custom_call_target="tpu_custom_call" | custom-call | tf_op jit(solution)/shard_map/pallas_call | solution.py:375
  39.4 1.5 %copy.6 = f32[32,1,384]{2,1,0:T(1,128)} copy(f32[32,1,384]{2,0,1:T(8,128)} %bitcast.4) | data formatting | bytes 98304 | tf_op jit(solution)/shard_map/reshape | solution.py:412

commit v3 on v2

--- a/solution.py
+++ b/solution.py
@@ -37,7 +37,7 @@
     part_in,
     z_out,
     z_in,
-    full_ref,
+    sum_ref,
     local_sem,
     sky_sem,
     tap_sem,
@@ -164,8 +164,8 @@
             for i, d in enumerate(devices)
         ]
 
+    tile_copies = [send(tiles_ref, tile_in.at[y + 1], tile_sem, i, d) for i, d in enumerate(y_ids)]
     pix_copies = [send(pixels_ref, pix_all.at[y + 1], pix_sem, i, d) for i, d in enumerate(y_ids)]
-    tile_copies = [send(tiles_ref, tile_in.at[y + 1], tile_sem, i, d) for i, d in enumerate(y_ids)]
     halo_tiles = give(tiles_ref, tile_in.at[0], tile_sem, Y - 1, halo_ids)
     halo_pixels = give(pixels_ref, pix_all.at[0], pix_sem, Y - 1, halo_ids)
     tap_copies = give(taps_ref, taps_all.at[sim], tap_sem, 0, tap_ids)
@@ -320,8 +320,11 @@
             (((1,), (1,)), ((), ())),
             preferred_element_type=jnp.float32,
         )
-    for k in range(wafer_count * groups):
-        part_ref[k // groups, k % groups] = part[k * share : (k + 1) * share]
+    for k in range(wafer_count):
+        for j in range(groups):
+            for sky in range(share):
+                at, to = (k * groups + j) * share + sky, sky * groups + j
+                part_ref[k, to // share, to % share : to % share + 1] = part[at : at + 1]
 
     copies = [send(part_ref.at[k], part_in.at[i], w_sem, i, d) for i, (k, d) in enumerate(zip(ws, w_ids))]
     wait_all(copies)
@@ -339,12 +342,13 @@
     total = jnp.zeros_like(total)
     for k in range(z_count):
         total += z_in[(z - k + z_count - 1) % z_count]
-    full_ref[y] = total
-
-    wait_all([send(full_ref.at[y], full_ref.at[y], g_sem, i, d) for i, d in enumerate(y_ids)])
-    for k in range(Y):
-        for j in range(panels):
-            out_ref[k * share : (k + 1) * share, j * LANES : (j + 1) * LANES] = full_ref[k, j]
+    sum_ref[...] = total
+
+    copies = [send(sum_ref, out_ref.at[y], g_sem, i, d) for i, d in enumerate(y_ids)]
+    own = pltpu.make_async_copy(sum_ref, out_ref.at[y], local_sem.at[1])
+    own.start()
+    own.wait()
+    wait_all(copies)
 
     for copy in sends:
         copy.wait_send()
@@ -374,9 +378,9 @@
         sems = lambda n: pltpu.SemaphoreType.DMA((2, n))
         maps = pl.pallas_call(
             functools.partial(kernel, (tm_count, wafer_count)),
-            out_shape=jax.ShapeDtypeStruct((skies, pixel_count), f32),
+            out_shape=jax.ShapeDtypeStruct((Y,) + piece, f32),
             in_specs=[hbm] * 5,
-            out_specs=pl.BlockSpec(memory_space=pltpu.VMEM),
+            out_specs=hbm,
             scratch_shapes=[
                 pltpu.VMEM((wafer_count, 16, pixel_count), bf16),
                 pltpu.VMEM((wafer_count, 16 // share, share, pixel_count), f32),
@@ -393,7 +397,7 @@
                 pltpu.VMEM((wafer_count - 1,) + piece, f32),
                 pltpu.VMEM(piece, f32),
                 pltpu.VMEM((z_count,) + piece, f32),
-                pltpu.VMEM((Y,) + piece, f32),
+                pltpu.VMEM(piece, f32),
                 pltpu.SemaphoreType.DMA((5,)),
                 sems(wafer_count - 1),
                 sems(z_count),

time: 41.1 us -> 39.9 us (0.971)
  Pallas kernels: 38.8 us -> 37.4 us
    reshape x1 -> x0, local copies, waits for them, and re-layouts: 1.47 us -> none  [per_device(): return maps.reshape(skies, 1, pixel_count)]
    unnamed x0 -> x1, local copies, waits for them, and re-layouts: none -> 1.44 us
    pallas_call x1, Pallas kernels: 38.8 us -> 37.4 us  [per_device(): pl.pallas_call(functools.partial(kernel, (tm_count, wafer_count)), out_sh...]
where the time goes in v3:
time: 39.9 us; the launch traced here: 39.5 us
  Pallas kernels  37.4 us (94%)
  local copies, waits for them, and re-layouts  1.44 us (4%)
  between operations  0.66 us (2%)
    pallas_call x1, Pallas kernels, per_device(): pl.pallas_call(functools.partial(kernel, (tm_count, wafer_count)), out_sh...  37.4 us
    unnamed x1, local copies, waits for them, and re-layouts  1.44 us

profile of v3, /device:TPU:1, one launch (start us, length us, event | category | flops | bytes accessed | tf_op | source)
XLA Modules:
  0.0 39.5 jit_solution(12902912609646919024)
XLA Ops:
  0.7 37.4 %shard_map.55 = f32[8,3,4,128]{3,2,1,0:T(4,128)} custom-call(bf16[32,384]{1,0:T(8,128)(2,1)} %bitcast.5, bf16[1,1024]{1,0:T(2,128)(2,1)} %taps_ref.1, f32[1,1]{1,0:T(1,128)} %bitcast.3.weights_ref, s32[1,2048]{1,0:T(1,128)} %pixels_ref.1, s32[1,16]{1,0:T(1,128)} %tiles_ref.1), custom_call_target="tpu_custom_call" | custom-call | tf_op jit(solution)/shard_map/pallas_call | solution.py:379
  38.1 1.4 %copy.9 = f32[32,1,384]{2,1,0:T(1,128)} copy(f32[32,1,384]{2,1,0:T(1,128)} %bitcast.4) | data formatting | bytes 98304

commit v4 on v3

--- a/solution.py
+++ b/solution.py
@@ -67,7 +67,7 @@
     y, z = tm % Y, tm // Y
     per_half = half_rows // share
 
-    ws = [(wafer + k) % wafer_count for k in range(1, wafer_count)]
+    ws = [(wafer + k) % wafer_count for k in (4, 5, 3, 2, 6, 1, 7)]
     ys = [(y + k) % Y for k in Y_STEPS]
     zs = [(z + k) % z_count for k in range(1, z_count)]
     w_ids = [{"wafer": k} for k in ws]
@@ -327,9 +327,9 @@
                 part_ref[k, to // share, to % share : to % share + 1] = part[at : at + 1]
 
     copies = [send(part_ref.at[k], part_in.at[i], w_sem, i, d) for i, (k, d) in enumerate(zip(ws, w_ids))]
-    wait_all(copies)
     total = part_ref[wafer]
-    for i in range(wafer_count - 1):
+    for i in reversed(range(wafer_count - 1)):
+        copies[i].wait_recv()
         total += part_in[i]
     z_out[...] = total
 

time: 39.9 us -> 39.7 us (level)
  no operation moved by 1% of the time
where the time goes in v4:
time: 39.7 us; the launch traced here: 39.4 us
  Pallas kernels  37.3 us (94%)
  local copies, waits for them, and re-layouts  1.44 us (4%)
  between operations  0.66 us (2%)
    pallas_call x1, Pallas kernels, per_device(): pl.pallas_call(functools.partial(kernel, (tm_count, wafer_count)), out_sh...  37.3 us
    unnamed x1, local copies, waits for them, and re-layouts  1.44 us

profile of v4, /device:TPU:1, one launch (start us, length us, event | category | flops | bytes accessed | tf_op | source)
XLA Modules:
  0.0 39.4 jit_solution(1439597593120171404)
XLA Ops:
  0.7 37.3 %shard_map.55 = f32[8,3,4,128]{3,2,1,0:T(4,128)} custom-call(bf16[32,384]{1,0:T(8,128)(2,1)} %bitcast.5, bf16[1,1024]{1,0:T(2,128)(2,1)} %taps_ref.1, f32[1,1]{1,0:T(1,128)} %bitcast.3.weights_ref, s32[1,2048]{1,0:T(1,128)} %pixels_ref.1, s32[1,16]{1,0:T(1,128)} %tiles_ref.1), custom_call_target="tpu_custom_call" | custom-call | tf_op jit(solution)/shard_map/pallas_call | solution.py:379
  37.9 1.4 %copy.9 = f32[32,1,384]{2,1,0:T(1,128)} copy(f32[32,1,384]{2,1,0:T(1,128)} %bitcast.4) | data formatting | bytes 98304

commit v5 on v3

--- a/solution.py
+++ b/solution.py
@@ -164,8 +164,10 @@
             for i, d in enumerate(devices)
         ]
 
-    tile_copies = [send(tiles_ref, tile_in.at[y + 1], tile_sem, i, d) for i, d in enumerate(y_ids)]
-    pix_copies = [send(pixels_ref, pix_all.at[y + 1], pix_sem, i, d) for i, d in enumerate(y_ids)]
+    tile_copies, pix_copies = [], []
+    for i, d in enumerate(y_ids):
+        tile_copies.append(send(tiles_ref, tile_in.at[y + 1], tile_sem, i, d))
+        pix_copies.append(send(pixels_ref, pix_all.at[y + 1], pix_sem, i, d))
     halo_tiles = give(tiles_ref, tile_in.at[0], tile_sem, Y - 1, halo_ids)
     halo_pixels = give(pixels_ref, pix_all.at[0], pix_sem, Y - 1, halo_ids)
     tap_copies = give(taps_ref, taps_all.at[sim], tap_sem, 0, tap_ids)

time: 39.9 us -> 39.9 us (level)
  no operation moved by 1% of the time
where the time goes in v5:
time: 39.9 us; the launch traced here: 39.5 us
  Pallas kernels  37.4 us (94%)
  local copies, waits for them, and re-layouts  1.44 us (4%)
  between operations  0.66 us (2%)
    pallas_call x1, Pallas kernels, per_device(): pl.pallas_call(functools.partial(kernel, (tm_count, wafer_count)), out_sh...  37.4 us
    unnamed x1, local copies, waits for them, and re-layouts  1.44 us

profile of v5, /device:TPU:1, one launch (start us, length us, event | category | flops | bytes accessed | tf_op | source)
XLA Modules:
  0.0 39.5 jit_solution(16398207699189095352)
XLA Ops:
  0.7 37.4 %shard_map.55 = f32[8,3,4,128]{3,2,1,0:T(4,128)} custom-call(bf16[32,384]{1,0:T(8,128)(2,1)} %bitcast.5, bf16[1,1024]{1,0:T(2,128)(2,1)} %taps_ref.1, f32[1,1]{1,0:T(1,128)} %bitcast.3.weights_ref, s32[1,2048]{1,0:T(1,128)} %pixels_ref.1, s32[1,16]{1,0:T(1,128)} %tiles_ref.1), custom_call_target="tpu_custom_call" | custom-call | tf_op jit(solution)/shard_map/pallas_call | solution.py:381
  38.1 1.4 %copy.9 = f32[32,1,384]{2,1,0:T(1,128)} copy(f32[32,1,384]{2,1,0:T(1,128)} %bitcast.4) | data formatting | bytes 98304
